TPU v7x, 32 devices: a whole 2x2x4 slice. The times are simulated.
32 devices in a mesh: groups: 2 (over y), db: 4 (over z), sub: 2 (over x), rep: 2 (over core).
Axes of the slice: x: 2, y: 2, z: 4, core: 2. Of those that a mesh axis runs over, the one named last changes fastest.
Arguments:
- query_pooled: bfloat16 [128, 1280], P(('groups', 'db')), parts along dimension 0, may hold values from -48 to 48
- db_pooled: bfloat16 [8192, 1280], P(('groups', 'db', 'sub', 'rep')), parts along dimension 0, may hold values from -48 to 48
- query_res: bfloat16 [64, 64, 1280], P(('groups', 'db', 'sub', 'rep')), parts along dimension 0, may hold values from -48 to 48
- query_len: int32 [64], P(('groups', 'db', 'sub', 'rep')), parts along dimension 0, may hold values from 1 to 64, 1280 in all
- db_res: bfloat16 [128, 64, 1280], P(('groups', 'db', 'sub', 'rep')), parts along dimension 0, may hold values from -48 to 48
- db_len: int32 [128], P(('groups', 'db', 'sub', 'rep')), parts along dimension 0, may hold values from 1 to 64, 2560 in all
- cand_seq: int32 [128], P(('groups', 'db', 'sub', 'rep')), parts along dimension 0, may hold values from 0 to 3
- cand_dest: int32 [128, 1], P(('groups', 'db', 'sub', 'rep')), parts along dimension 0, may hold values from 0 to 3; in each aligned block of 4 rows (0 to 3, 4 to 7, ...) at most 2 rows name the same one
- cand_query: int32 [128], P(('groups', 'db', 'sub', 'rep')), parts along dimension 0, may hold values from 0 to 1
Outputs:
- coarse: float32 [128], P(('groups', 'db')), parts along dimension 0
- align_score: float32 [128], P(('groups', 'db', 'sub', 'rep')), parts along dimension 0
There are 2 independent parts, one for each index of `groups`. A program takes and returns all parts, laid end to end along the dimension named above; each array names one. Nothing has to cross between parts.
Inputs may be any that keep to these rules, and one draw needn't show every extreme that they name: `cand_dest`: among the 4 candidates of one device, at most 2 name the same db index, and in every draw some device has exactly 2 naming one index. `query_len`: in each part along groups the 32 lengths sum to 1280, and some query has exactly 64 residues. `db_len`: in each part along groups the 64 lengths sum to 2560, and some sequence has exactly 64 residues.
All inputs are finite; a program needn't handle non-finite values.
Results may differ from a plain program's by a relative error of at most 0.0003.
Values may be sent and summed in bfloat16 or wider, within the bound.
A program may use at most 128 MiB of HBM per device.

v0:
```python
import jax
import jax.numpy as jnp
from jax import lax
from jax.sharding import PartitionSpec as P


def joined(part, axis, combine):
    gathered = jax.tree.map(lambda a: lax.all_gather(a, axis), part)

    def take(source):
        return jax.tree.map(lambda a: lax.dynamic_index_in_dim(a, source, 0, False), gathered)

    return lax.fori_loop(
        1, lax.axis_size(axis), lambda source, state: combine(state, take(source)), take(0)
    )


def join_stats(first, second):
    highest = jnp.maximum(first[0], second[0])
    summed = first[1] * jnp.exp(first[0] - highest) + second[1] * jnp.exp(second[0] - highest)
    return (highest, summed)


def soft_align(queries, blocks, query_lengths, block_lengths):
    factor = queries.shape[-1] ** (-0.5)
    similar = (
        jnp.einsum("nid,njd->nij", queries, blocks, preferred_element_type=jnp.float32) * factor
    )
    row_index = lax.broadcasted_iota(jnp.int32, similar.shape, 1)
    column_index = lax.broadcasted_iota(jnp.int32, similar.shape, 2)
    rows_valid = row_index < query_lengths[:, None, None]
    columns_valid = column_index < block_lengths[:, None, None]
    across = jnp.where(columns_valid, similar, -1e30)
    across_top = jnp.max(across, axis=2, keepdims=True)
    across_weight = jnp.where(columns_valid, jnp.exp(across - across_top), 0.0)
    across_weight = across_weight / jnp.sum(across_weight, axis=2, keepdims=True)
    down = jnp.where(rows_valid, similar, -1e30)
    down_top = jnp.max(down, axis=1, keepdims=True)
    down_weight = jnp.where(rows_valid, jnp.exp(down - down_top), 0.0)
    down_weight = down_weight / jnp.sum(down_weight, axis=1, keepdims=True)
    both_valid = rows_valid & columns_valid
    row_part = jnp.sum(jnp.where(both_valid, across_weight * similar, 0.0), axis=(1, 2))
    column_part = jnp.sum(jnp.where(both_valid, down_weight * similar, 0.0), axis=(1, 2))
    return 0.5 * row_part / query_lengths.astype(
        jnp.float32
    ) + 0.5 * column_part / block_lengths.astype(jnp.float32)


def body(
    query_pooled, db_pooled, query_res, query_len, db_res, db_len, cand_seq, cand_dest, cand_query
):
    factor = db_pooled.shape[1] ** (-0.5)
    per_owner = query_pooled.shape[0]
    similar = (
        lax.dot_general(
            lax.all_gather(query_pooled, "db", axis=0, tiled=True),
            db_pooled,
            (((1,), (1,)), ((), ())),
            preferred_element_type=jnp.float32,
        )
        * factor
    )
    piece_top = jnp.max(similar, axis=1)
    piece_sum = jnp.sum(jnp.exp(similar - piece_top[:, None]), axis=1)
    highest = piece_top
    summed = piece_sum
    highest, summed = (highest, summed)
    highest, summed = joined((highest, summed), ("db", "sub", "rep"), join_stats)
    offset = lax.axis_index("db") * per_owner
    own_top = lax.dynamic_slice_in_dim(highest, offset, per_owner, 0)
    own_sum = lax.dynamic_slice_in_dim(summed, offset, per_owner, 0)
    coarse = own_top + jnp.log(own_sum)
    target = cand_dest[:, 0]
    gathered, gathered_len = (
        lax.all_gather(query_res, "db", axis=0, tiled=True),
        lax.all_gather(query_len, "db", axis=0, tiled=True),
    )
    chosen_ids = target * query_res.shape[0] + cand_query
    align_score = soft_align(
        gathered[chosen_ids], db_res[cand_seq], gathered_len[chosen_ids], db_len[cand_seq]
    )
    return (coarse, align_score)


def solution(mesh):
    in_specs = (
        P(("groups", "db"), None),
        P(("groups", "db", "sub", "rep"), None),
        P(("groups", "db", "sub", "rep"), None, None),
        P(("groups", "db", "sub", "rep")),
        P(("groups", "db", "sub", "rep"), None, None),
        P(("groups", "db", "sub", "rep")),
        P(("groups", "db", "sub", "rep")),
        P(("groups", "db", "sub", "rep"), None),
        P(("groups", "db", "sub", "rep")),
    )
    out_specs = (P(("groups", "db")), P(("groups", "db", "sub", "rep")))
    return jax.shard_map(body, mesh=mesh, in_specs=in_specs, out_specs=out_specs, check_vma=False)
```

profile of v0, /device:TPU:0, one launch (start us, length us, event | category | flops | bytes accessed | tf_op | source)
XLA Modules:
  0.0 79.2 jit_solution(13577881432845007369)
XLA Ops:
  7.2 0.0 copy-start
  7.2 0.0 copy-start.7
  7.2 0.0 copy-start.6
  7.2 0.0 copy-start.2
  7.2 0.0 copy-start.4
  7.2 0.0 copy-start.3
  7.2 0.0 copy-start.5
  7.2 0.0 all-gather.4.cloned.1.call-start
  7.3 0.7 all-gather.4.cloned.1.call-update
  8.0 0.0 copy-start.1
  8.0 15.4 %all_gather.21 = bf16[64,1280]{1,0:T(8,128)(2,1)S(1)} all-gather(bf16[16,1280]{1,0:T(8,128)(2,1)} %param.11), channel_id=1, replica_groups=mesh['groups'=2,'db'=4,'sub'=2,'rep'=2] {'db'}, dimensions={0}, use_global_device_ids=true | all-gather | bytes 204800 | tf_op jit(solution)/shard_map/all_gather | solution.py:56
  23.4 1.5 %fusion.43 = (f32[64]{0:T(128)S(1)}, f32[64,256]{1,0:T(8,128)S(1)}) fusion(bf16[64,1280]{1,0:T(8,128)(2,1)S(1)} %all_gather.21, bf16[256,1280]{1,0:T(8,128)(2,1)} %param.12), kind=kOutput, calls=%fused_computation.55 | convolution fusion | flops 41975744 | bytes 884992 | tf_op jit(solution)/shard_map/dot_general | solution.py:55
  24.9 0.2 exponential_reduce_fusion
  25.1 0.0 copy-done.7
  25.1 0.6 dynamic-slice
  26.4 0.2 dynamic-update-slice
  26.6 0.2 dynamic-update-slice.1
  26.8 31.7 %all-reduce.3 = (f32[1024]{0:T(1024)S(1)}, f32[1024]{0:T(1024)S(1)}) all-reduce(f32[1024]{0:T(1024)S(1)} %dynamic-update-slice, f32[1024]{0:T(1024)S(1)} %dynamic-update-slice.1), channel_id=2, replica_groups=mesh['groups'=2,'db'=4,'sub'=2,'rep'=2] {'db','sub','rep'}, use_global_device_ids=true, to_apply=%add | all-reduce | flops 2048 | bytes 16384
  58.5 0.1 reshape.45
  58.6 0.1 reshape.46
  58.6 0.0 copy-done.6
  58.6 0.6 dynamic-slice.2
  59.9 0.0 copy-done.2
  59.9 0.2 dynamic-update-slice.2
  60.1 5.6 %all-reduce.2 = s32[8]{0:T(128)S(1)} all-reduce(s32[8]{0:T(128)S(1)} %dynamic-update-slice.2), channel_id=1, replica_groups=mesh['groups'=2,'db'=4,'sub'=2,'rep'=2] {'db'}, use_global_device_ids=true, to_apply=%add.2 | all-reduce | flops 8 | bytes 64
  65.7 0.0 copy-done.4
  65.7 0.0 copy-done.3
  65.8 0.0 copy-done.5
  65.8 0.0 copy-done
  65.8 0.6 gather_fusion.3
  66.4 0.0 copy-done.1
  66.4 0.6 gather_fusion.1
  67.0 0.6 gather_fusion
  67.7 0.7 while.17
  68.3 0.6 log_add_fusion
  68.9 0.0 all-gather.4.cloned.1.call-done
  69.0 1.9 %gather_fusion.2 = bf16[4,64,1280]{2,1,0:T(8,128)(2,1)S(1)} fusion(bf16[8,64,1280]{2,1,0:T(8,128)(2,1)} %all-gather.4.cloned.1.call-done, s32[1024]{0:T(1024)S(1)} %pad_clamp_fusion.1), kind=kCustom, calls=%fused_computation.2 | custom fusion | bytes 1310736 | tf_op jit(solution)/shard_map/gather | solution.py:80
  70.9 0.3 convolution_multiply_fusion
  71.2 0.3 fusion.44
  71.4 0.4 fusion.47
  71.9 0.5 divide_add_fusion
  (24 shorter events, 0.4 us)
Async XLA Ops:
  7.2 58.6 %copy-start = (bf16[4,64,1280]{2,1,0:T(8,128)(2,1)S(1)}, bf16[4,64,1280]{2,1,0:T(8,128)(2,1)}, u32[]{:S(2)}) copy-start(bf16[4,64,1280]{2,1,0:T(8,128)(2,1)} %param.15) | copy-start | bytes 1966084
  7.2 17.9 %copy-start.7 = (u32[32]{0:T(128)S(1)}, u32[32]{0:T(128)}, u32[]{:S(2)}) copy-start(u32[32]{0:T(128)} %constant.83) | copy-start | bytes 388
  7.2 51.5 %copy-start.6 = (u32[32]{0:T(128)S(1)}, u32[32]{0:T(128)}, u32[]{:S(2)}) copy-start(u32[32]{0:T(128)} %constant.93) | copy-start | bytes 388
  7.2 52.7 %copy-start.2 = (s32[2]{0:T(128)S(1)}, s32[2]{0:T(128)}, u32[]{:S(2)}) copy-start(s32[2]{0:T(128)} %param.14) | copy-start | bytes 28
  7.2 58.5 %copy-start.4 = (s32[4,1]{0,1:T(1,128)S(1)}, s32[4,1]{0,1:T(1,128)}, u32[]{:S(2)}) copy-start(s32[4,1]{0,1:T(1,128)} %param.18) | copy-start | bytes 52
  7.2 58.5 %copy-start.3 = (s32[4]{0:T(128)S(1)}, s32[4]{0:T(128)}, u32[]{:S(2)}) copy-start(s32[4]{0:T(128)} %param.19) | copy-start | bytes 52
  7.2 58.5 %copy-start.5 = (s32[4]{0:T(128)S(1)}, s32[4]{0:T(128)}, u32[]{:S(2)}) copy-start(s32[4]{0:T(128)} %param.17) | copy-start | bytes 52
  7.2 61.7 %all-gather.4.cloned.1.call-start = ((), (), s32[]{:S(2)}) async-start(), calls=%async_computation | async-start | bytes 1638400 | tf_op jit(solution)/shard_map/all_gather | solution.py:75
  8.0 58.4 %copy-start.1 = (s32[4]{0:T(128)S(1)}, s32[4]{0:T(128)}, u32[]{:S(2)}) copy-start(s32[4]{0:T(128)} %param.16) | copy-start | bytes 52
Sparse Core Ops, SparseCore 0:
  9.6 35.9 all-gather.3
where the time goes:
time: 79.5 us; the launch traced here: 79.2 us
  blocking collectives  52.6 us (66%)
  between operations  15.5 us (19%)
  local copies, waits for them, and re-layouts  5.83 us (7%)
  other arithmetic  2.42 us (3%)
  matrix products  1.85 us (2%)
    unnamed x2, blocking collectives  37.3 us
    all_gather x1, blocking collectives, body(): lax.all_gather(query_pooled, 'db', axis=0, tiled=True)  15.4 us
    unnamed x24, local copies, waits for them, and re-layouts  1.92 us
    gather x1, local copies, waits for them, and re-layouts, body(): gathered[chosen_ids]  1.9 us
  transfers between devices with their start and end apart: 1, of which 0 were waited for; matrix products, arithmetic and copies ran while one was open for 8% of the time, Pallas kernels for 0%

commit v1 on v0

v1 whole, which is shorter than its diff:
```python
import functools

import jax
import jax.numpy as jnp
from jax import lax
from jax.experimental import pallas as pl
from jax.experimental.pallas import tpu as pltpu
from jax.sharding import PartitionSpec as P

MESH = pl.DeviceIdType.MESH
LANES = 128


def fold(pieces):
    top = functools.reduce(jnp.maximum, [p[0] for p in pieces])
    total = sum(p[1] * jnp.exp(p[0] - top) for p in pieces)
    return top, total


def align(query, block, lq_row, lt, factor):
    similar = lax.dot_general(
        query, block, (((1,), (1,)), ((), ())), preferred_element_type=jnp.float32
    ) * factor
    rows = lax.broadcasted_iota(jnp.int32, similar.shape, 0) < lq_row[:, : similar.shape[1]]
    columns = lax.broadcasted_iota(jnp.int32, similar.shape, 1) < lt
    across = jnp.where(columns, similar, -1e30)
    weight = jnp.where(columns, jnp.exp(across - jnp.max(across, axis=1, keepdims=True)), 0.0)
    row_part = jnp.sum(weight * similar, axis=1, keepdims=True) / jnp.sum(
        weight, axis=1, keepdims=True
    )
    row_part = jnp.sum(jnp.where(rows[:, :1], row_part, 0.0), axis=0, keepdims=True)
    down = jnp.where(rows, similar, -1e30)
    weight = jnp.where(rows, jnp.exp(down - jnp.max(down, axis=0, keepdims=True)), 0.0)
    column_part = jnp.sum(weight * similar, axis=0, keepdims=True) / jnp.sum(
        weight, axis=0, keepdims=True
    )
    column_part = jnp.sum(jnp.where(columns[:1], column_part, 0.0), axis=1, keepdims=True)
    lq = lq_row[:, :1].astype(jnp.float32)
    return 0.5 * row_part / lq + 0.5 * column_part / lt.astype(jnp.float32)


def kernel(
    n, n_sub, n_rep,
    qp_ref, dbp_hbm, qres_hbm, qlen_ref, dbres_hbm, dblen_ref, seq_ref, dest_ref, cq_ref,
    coarse_ref, score_ref,
    qp_all, dbp, dbres, res_all, len_all, stat, stat_db, stat_node,
    local_sem, qp_send, qp_recv, len_send, len_recv, res_send, res_recv,
    a_send, a_recv, b_send, b_recv,
):
    db, sub, rep = lax.axis_index("db"), lax.axis_index("sub"), lax.axis_index("rep")
    node = n_sub * n_rep
    spot = sub * n_rep + rep
    per_owner, width = qp_ref.shape
    held = qres_hbm.shape[0]
    factor = width ** (-0.5)

    def on_line(i):
        return lax.rem(db + i, n)

    def in_node(i):
        other = lax.rem(spot + i, node)
        return other, {"sub": other // n_rep, "rep": lax.rem(other, n_rep)}

    local = [
        pltpu.make_async_copy(qres_hbm, res_all.at[pl.ds(db * held, held)], local_sem.at[0]),
        pltpu.make_async_copy(dbp_hbm, dbp, local_sem.at[1]),
        pltpu.make_async_copy(dbres_hbm, dbres, local_sem.at[2]),
    ]
    for copy in local:
        copy.start()
    barrier = pltpu.get_barrier_semaphore()
    for i in range(1, n):
        pl.semaphore_signal(barrier, inc=1, device_id={"db": on_line(i)}, device_id_type=MESH)
    for i in range(1, node):
        pl.semaphore_signal(barrier, inc=1, device_id=in_node(i)[1], device_id_type=MESH)
    qp_all[db] = qp_ref[...]
    for q in range(held):
        len_all[db * held + q] = jnp.full(len_all.shape[1:], qlen_ref[q], jnp.int32)
    pl.semaphore_wait(barrier, n - 1 + node - 1)

    def qp_copy(source, target, i):
        return pltpu.make_async_remote_copy(
            src_ref=qp_all.at[source], dst_ref=qp_all.at[source],
            send_sem=qp_send.at[i], recv_sem=qp_recv.at[source],
            device_id={"db": target}, device_id_type=MESH,
        )

    def len_copy(source, target, i):
        part = len_all.at[pl.ds(source * held, held)]
        return pltpu.make_async_remote_copy(
            src_ref=part, dst_ref=part,
            send_sem=len_send.at[i], recv_sem=len_recv.at[source],
            device_id={"db": target}, device_id_type=MESH,
        )

    def res_copy(source, q, step, side):
        part = res_all.at[source * held + q]
        return pltpu.make_async_remote_copy(
            src_ref=part, dst_ref=part,
            send_sem=res_send.at[side, step, q], recv_sem=res_recv.at[source, q],
            device_id={"db": lax.rem(db + (2 * side - 1) + n, n)}, device_id_type=MESH,
        )

    def a_copy(source, owner, i):
        return pltpu.make_async_remote_copy(
            src_ref=stat.at[owner], dst_ref=stat_db.at[source],
            send_sem=a_send.at[i], recv_sem=a_recv.at[source],
            device_id={"db": owner}, device_id_type=MESH,
        )

    def b_copy(source, target, i):
        return pltpu.make_async_remote_copy(
            src_ref=stat_node.at[source], dst_ref=stat_node.at[source],
            send_sem=b_send.at[i], recv_sem=b_recv.at[source],
            device_id=target, device_id_type=MESH,
        )

    for i in range(1, n):
        qp_copy(db, on_line(i), i).start()
    local[0].wait()

    def own(side):
        for q in range(held):
            res_copy(db, q, 0, side).start()

    pl.when(db < n - 1)(lambda: own(1))
    pl.when(db > 0)(lambda: own(0))
    for i in range(1, n):
        len_copy(db, on_line(i), i).start()

    local[1].wait()
    for i in range(1, n):
        qp_copy(on_line(i), db, i).wait_recv()
    similar = lax.dot_general(
        qp_all[...].reshape(n * per_owner, width), dbp[...], (((1,), (1,)), ((), ())),
        preferred_element_type=jnp.float32,
    ) * factor
    top = jnp.max(similar, axis=1, keepdims=True)
    total = jnp.sum(jnp.exp(similar - top), axis=1, keepdims=True)
    for k in range(n):
        rows = slice(k * per_owner, (k + 1) * per_owner)
        stat[k, 0] = jnp.broadcast_to(top[rows], (per_owner, LANES))
        stat[k, 1] = jnp.broadcast_to(total[rows], (per_owner, LANES))
    for i in range(1, n):
        a_copy(db, on_line(i), i).start()
    stat_db[db] = stat[db]

    def relay(step):
        for side in (1, 0):
            source = db - step if side else db + step
            valid = source >= 0 if side else source < n
            more = db < n - 1 if side else db > 0

            @pl.when(valid)
            def _():
                for q in range(held):
                    res_copy(source, q, step, side).wait_recv()

                    @pl.when(more)
                    def _():
                        res_copy(source, q, step, side).start()

    def join_db():
        for i in range(1, n):
            a_copy(on_line(i), db, i).wait_recv()
        top, total = fold([(stat_db[k, 0], stat_db[k, 1]) for k in range(n)])
        stat_node[spot, 0] = top
        stat_node[spot, 1] = total
        for i in range(1, node):
            b_copy(spot, in_node(i)[1], i).start()

    def join_node():
        for i in range(1, node):
            b_copy(in_node(i)[0], in_node(i)[1], i).wait_recv()
        top, total = fold([(stat_node[k, 0], stat_node[k, 1]) for k in range(node)])
        coarse_ref[...] = top + jnp.log(total)

    relay(1)
    join_db()
    if n > 2:
        relay(2)
    join_node()
    if n > 3:
        lax.fori_loop(3, n, lambda step, _: (relay(step), 0)[1], 0)
    local[2].wait()
    for i in range(1, n):
        len_copy(on_line(i), db, i).wait_recv()

    def score(c, _):
        chosen = dest_ref[c, 0] * held + cq_ref[c]
        seq = seq_ref[c]
        value = align(res_all[chosen], dbres[seq], len_all[chosen][:1], dblen_ref[seq], factor)
        score_ref[pl.ds(c, 1), :] = jnp.broadcast_to(value, (1, LANES))
        return 0

    count = score_ref.shape[0]
    if count <= 8:
        for c in range(count):
            score(c, 0)
    else:
        lax.fori_loop(0, count, score, 0)

    for i in range(1, n):
        qp_copy(db, on_line(i), i).wait_send()
        len_copy(db, on_line(i), i).wait_send()
        a_copy(db, on_line(i), i).wait_send()
    for i in range(1, node):
        b_copy(spot, in_node(i)[1], i).wait_send()

    def drain(step, _):
        for side in (1, 0):
            source = db - step if side else db + step
            more = (db < n - 1) & (source >= 0) if side else (db > 0) & (source < n)

            @pl.when(more)
            def _():
                for q in range(held):
                    res_copy(source, q, step, side).wait_send()

        return 0

    lax.fori_loop(0, n, drain, 0)


def body(
    n, n_sub, n_rep,
    query_pooled, db_pooled, query_res, query_len, db_res, db_len, cand_seq, cand_dest, cand_query,
):
    per_owner, width = query_pooled.shape
    held, longest, _ = query_res.shape
    count = cand_seq.shape[0]
    node = n_sub * n_rep
    vmem, smem, anywhere = (
        pl.BlockSpec(memory_space=pltpu.VMEM),
        pl.BlockSpec(memory_space=pltpu.SMEM),
        pl.BlockSpec(memory_space=pl.ANY),
    )
    dma = pltpu.SemaphoreType.DMA
    coarse, score = pl.pallas_call(
        functools.partial(kernel, n, n_sub, n_rep),
        out_shape=(
            jax.ShapeDtypeStruct((per_owner, LANES), jnp.float32),
            jax.ShapeDtypeStruct((count, LANES), jnp.float32),
        ),
        in_specs=[vmem, anywhere, anywhere, smem, anywhere, smem, smem, smem, smem],
        out_specs=(vmem, vmem),
        scratch_shapes=[
            pltpu.VMEM((n, per_owner, width), jnp.bfloat16),
            pltpu.VMEM(db_pooled.shape, jnp.bfloat16),
            pltpu.VMEM(db_res.shape, jnp.bfloat16),
            pltpu.VMEM((n * held, longest, width), jnp.bfloat16),
            pltpu.VMEM((n * held, 8, LANES), jnp.int32),
            pltpu.VMEM((n, 2, per_owner, LANES), jnp.float32),
            pltpu.VMEM((n, 2, per_owner, LANES), jnp.float32),
            pltpu.VMEM((node, 2, per_owner, LANES), jnp.float32),
            dma((3,)),
            dma((n,)), dma((n,)), dma((n,)), dma((n,)),
            dma((2, n, held)), dma((n, held)),
            dma((n,)), dma((n,)), dma((node,)), dma((node,)),
        ],
        compiler_params=pltpu.CompilerParams(
            collective_id=0, has_side_effects=True, vmem_limit_bytes=40 * 2**20
        ),
    )(
        query_pooled, db_pooled, query_res, query_len, db_res, db_len,
        cand_seq, cand_dest, cand_query,
    )
    return coarse[:, 0], score[:, 0]


def solution(mesh):
    every = ("groups", "db", "sub", "rep")
    in_specs = (
        P(("groups", "db"), None), P(every, None), P(every, None, None), P(every),
        P(every, None, None), P(every), P(every), P(every, None), P(every),
    )
    out_specs = (P(("groups", "db")), P(every))
    sizes = [mesh.shape[a] for a in ("db", "sub", "rep")]
    return jax.shard_map(
        functools.partial(body, *sizes), mesh=mesh, in_specs=in_specs, out_specs=out_specs,
        check_vma=False,
    )
```

time: 79.5 us -> 41.3 us (0.52)
  blocking collectives: 52.6 us -> 0 us
  Pallas kernels: 0 us -> 34.4 us
  between operations: 15.5 us -> 0.69 us
  other arithmetic: 2.42 us -> 0 us
  matrix products: 1.85 us -> 0 us
    unnamed x2 -> x0, blocking collectives: 37.3 us -> none
    pallas_call x0 -> x1, Pallas kernels: none -> 34.4 us  [body(): pl.pallas_call(functools.partial(kernel, n, n_sub, n_rep), out_shape=(jax...]
    all_gather x1 -> x0, blocking collectives: 15.4 us -> none  [body(): lax.all_gather(query_pooled, 'db', axis=0, tiled=True)]
    gather x4 -> x0, local copies, waits for them, and re-layouts: 3.77 us -> none  [the longest x1 1.9 us: body(): gathered[chosen_ids]]
    unnamed x24 -> x17, local copies, waits for them, and re-layouts: 1.92 us -> 4.7 us
    dot_general x2 -> x0, matrix products: 1.85 us -> none  [the longest x1 1.54 us: body(): lax.dot_general(lax.all_gather(query_pooled, 'db', axis=0, tiled=True), d...]
    add x17 -> x0, other arithmetic: 1.53 us -> none  [the longest x1 0.6 us: body(): coarse = own_top + jnp.log(own_sum)]
    slice x0 -> x2, local copies, waits for them, and re-layouts: none -> 1.25 us  [body(): return (coarse[:, 0], score[:, 0])]
  transfers between devices with their start and end apart: 1 -> 0, of which waited for: 0 -> 0; matrix products, arithmetic and copies ran while one was open for 8% -> 0% of each run, Pallas kernels for 0% -> 0%
where the time goes in v1:
time: 41.3 us; the launch traced here: 41 us
  Pallas kernels  34.4 us (83%)
  local copies, waits for them, and re-layouts  5.95 us (14%)
  between operations  0.69 us (2%)
    pallas_call x1, Pallas kernels, body(): pl.pallas_call(functools.partial(kernel, n, n_sub, n_rep), out_shape=(jax...  34.4 us
    unnamed x17, local copies, waits for them, and re-layouts  4.7 us
    slice x2, local copies, waits for them, and re-layouts, body(): return (coarse[:, 0], score[:, 0])  1.25 us

profile of v1, /device:TPU:0, one launch (start us, length us, event | category | flops | bytes accessed | tf_op | source)
XLA Modules:
  0.0 41.0 jit_solution(4547781506702452426)
XLA Ops:
  0.6 0.0 copy-start.7
  0.6 0.0 copy-start.6
  0.7 0.0 copy-start.5
  0.7 0.0 copy-start.4
  0.7 0.8 %copy.12.dest_ref = s32[4,1]{1,0:T(4,128)S(1)} copy(s32[4,1]{0,1:T(1,128)} %param.16) | data formatting | bytes 32 | tf_op args[7]
  1.4 0.0 copy-done.7
  1.4 0.0 copy-done.6
  1.4 0.0 copy-done.5
  1.4 0.0 copy-done.4
  1.5 0.0 copy-start
  1.5 1.1 %copy-done = bf16[256,1280]{1,0:T(8,128)(2,1)S(1)} copy-done((bf16[256,1280]{1,0:T(8,128)(2,1)S(1)}, bf16[256,1280]{1,0:T(8,128)(2,1)}, u32[]{:S(2)}) %copy-start) | copy-done | bytes 655384
  2.5 0.0 copy-start.1
  2.5 1.1 %copy-done.1 = bf16[4,64,1280]{2,1,0:T(8,128)(2,1)S(1)} copy-done((bf16[4,64,1280]{2,1,0:T(8,128)(2,1)S(1)}, bf16[4,64,1280]{2,1,0:T(8,128)(2,1)}, u32[]{:S(2)}) %copy-start.1) | copy-done | bytes 655384
  3.6 0.0 copy-start.2
  3.6 1.0 %copy-done.2 = bf16[2,64,1280]{2,1,0:T(8,128)(2,1)S(1)} copy-done((bf16[2,64,1280]{2,1,0:T(8,128)(2,1)S(1)}, bf16[2,64,1280]{2,1,0:T(8,128)(2,1)}, u32[]{:S(2)}) %copy-start.2) | copy-done | bytes 327704
  4.6 0.0 copy-start.3
  4.6 0.8 %copy-done.3 = bf16[16,1280]{1,0:T(8,128)(2,1)S(1)} copy-done((bf16[16,1280]{1,0:T(8,128)(2,1)S(1)}, bf16[16,1280]{1,0:T(8,128)(2,1)}, u32[]{:S(2)}) %copy-start.3) | copy-done | bytes 40984
  5.4 34.4 %shard_map.104 = (f32[16,128]{1,0:T(8,128)S(1)}, f32[4,128]{1,0:T(4,128)S(1)}) custom-call(bf16[16,1280]{1,0:T(8,128)(2,1)S(1)} %copy-done.3, bf16[256,1280]{1,0:T(8,128)(2,1)S(1)} %copy-done, bf16[2,64,1280]{2,1,0:T(8,128)(2,1)S(1)} %copy-done.2, s32[2]{0:T(128)S(1)} %copy-done.4, bf16[4,64,1280]{2,1,0:T(8,128)(2,1)S(1)} %copy-done.1, s32[4]{0:T(128)S(1)} %copy-done.5, ...), custom_call_target="tpu_custom_call" | custom-call | tf_op jit(solution)/shard_map/pallas_call | solution.py:239
  39.7 0.6 %slice_reduce_fusion = f32[16]{0:T(128)} fusion(f32[16,128]{1,0:T(8,128)S(1)} %get-tuple-element.4), kind=kLoop, calls=%fused_computation | loop fusion | bytes 128 | tf_op jit(solution)/shard_map/slice | solution.py:268
  40.4 0.6 %slice_reduce_fusion.1 = f32[4]{0:T(128)} fusion(f32[4,128]{1,0:T(4,128)S(1)} %get-tuple-element.5), kind=kLoop, calls=%fused_computation.1 | loop fusion | bytes 32 | tf_op jit(solution)/shard_map/slice | solution.py:268
Async XLA Ops:
  0.6 0.8 %copy-start.7 = (s32[4]{0:T(128)S(1)}, s32[4]{0:T(128)}, u32[]{:S(2)}) copy-start(s32[4]{0:T(128)} %cq_ref.1) | copy-start | bytes 52
  0.6 0.8 %copy-start.6 = (s32[4]{0:T(128)S(1)}, s32[4]{0:T(128)}, u32[]{:S(2)}) copy-start(s32[4]{0:T(128)} %seq_ref.1) | copy-start | bytes 52
  0.7 0.8 %copy-start.5 = (s32[4]{0:T(128)S(1)}, s32[4]{0:T(128)}, u32[]{:S(2)}) copy-start(s32[4]{0:T(128)} %dblen_ref.1) | copy-start | bytes 52
  0.7 0.8 %copy-start.4 = (s32[2]{0:T(128)S(1)}, s32[2]{0:T(128)}, u32[]{:S(2)}) copy-start(s32[2]{0:T(128)} %qlen_ref.1) | copy-start | bytes 28
  1.5 1.1 %copy-start = (bf16[256,1280]{1,0:T(8,128)(2,1)S(1)}, bf16[256,1280]{1,0:T(8,128)(2,1)}, u32[]{:S(2)}) copy-start(bf16[256,1280]{1,0:T(8,128)(2,1)} %dbp_hbm.1) | copy-start | bytes 1966084
  2.5 1.1 %copy-start.1 = (bf16[4,64,1280]{2,1,0:T(8,128)(2,1)S(1)}, bf16[4,64,1280]{2,1,0:T(8,128)(2,1)}, u32[]{:S(2)}) copy-start(bf16[4,64,1280]{2,1,0:T(8,128)(2,1)} %dbres_hbm.1) | copy-start | bytes 1966084
  3.6 1.0 %copy-start.2 = (bf16[2,64,1280]{2,1,0:T(8,128)(2,1)S(1)}, bf16[2,64,1280]{2,1,0:T(8,128)(2,1)}, u32[]{:S(2)}) copy-start(bf16[2,64,1280]{2,1,0:T(8,128)(2,1)} %qres_hbm.1) | copy-start | bytes 983044
  4.6 0.8 %copy-start.3 = (bf16[16,1280]{1,0:T(8,128)(2,1)S(1)}, bf16[16,1280]{1,0:T(8,128)(2,1)}, u32[]{:S(2)}) copy-start(bf16[16,1280]{1,0:T(8,128)(2,1)} %qp_ref.1) | copy-start | bytes 122884

commit v2 on v1

--- a/solution.py
+++ b/solution.py
@@ -187,7 +187,7 @@
         len_copy(on_line(i), db, i).wait_recv()
 
     def score(c, _):
-        chosen = dest_ref[c, 0] * held + cq_ref[c]
+        chosen = dest_ref[c] * held + cq_ref[c]
         seq = seq_ref[c]
         value = align(res_all[chosen], dbres[seq], len_all[chosen][:1], dblen_ref[seq], factor)
         score_ref[pl.ds(c, 1), :] = jnp.broadcast_to(value, (1, LANES))
@@ -233,7 +233,7 @@
     vmem, smem, anywhere = (
         pl.BlockSpec(memory_space=pltpu.VMEM),
         pl.BlockSpec(memory_space=pltpu.SMEM),
-        pl.BlockSpec(memory_space=pl.ANY),
+        pl.BlockSpec(memory_space=pltpu.HBM),
     )
     dma = pltpu.SemaphoreType.DMA
     coarse, score = pl.pallas_call(
@@ -259,11 +259,11 @@
             dma((n,)), dma((n,)), dma((node,)), dma((node,)),
         ],
         compiler_params=pltpu.CompilerParams(
-            collective_id=0, has_side_effects=True, vmem_limit_bytes=40 * 2**20
+            collective_id=0, has_side_effects=True, vmem_limit_bytes=60 * 2**20
         ),
     )(
         query_pooled, db_pooled, query_res, query_len, db_res, db_len,
-        cand_seq, cand_dest, cand_query,
+        cand_seq, cand_dest[:, 0], cand_query,
     )
     return coarse[:, 0], score[:, 0]
 

time: 41.3 us -> 37.5 us (0.908)
  local copies, waits for them, and re-layouts: 5.95 us -> 1.95 us
    unnamed x17 -> x2, local copies, waits for them, and re-layouts: 4.7 us -> 0.01 us
    slice x2, local copies, waits for them, and re-layouts: 1.25 us -> 1.95 us  [body(): return (coarse[:, 0], score[:, 0])]
where the time goes in v2:
time: 37.5 us; the launch traced here: 37.3 us
  Pallas kernels  34.7 us (93%)
  local copies, waits for them, and re-layouts  1.95 us (5%)
  between operations  0.65 us (2%)
    pallas_call x1, Pallas kernels, body(): pl.pallas_call(functools.partial(kernel, n, n_sub, n_rep), out_shape=(jax...  34.7 us
    slice x2, local copies, waits for them, and re-layouts, body(): return (coarse[:, 0], score[:, 0])  1.95 us

profile of v2, /device:TPU:0, one launch (start us, length us, event | category | flops | bytes accessed | tf_op | source)
XLA Modules:
  0.0 37.3 jit_solution(14695219777802316471)
XLA Ops:
  0.6 34.7 %shard_map.104 = (f32[16,128]{1,0:T(8,128)}, f32[4,128]{1,0:T(4,128)}) custom-call(bf16[16,1280]{1,0:T(8,128)(2,1)} %qp_ref.1, bf16[256,1280]{1,0:T(8,128)(2,1)} %dbp_hbm.1, bf16[2,64,1280]{2,1,0:T(8,128)(2,1)} %qres_hbm.1, s32[2]{0:T(128)} %qlen_ref.1, bf16[4,64,1280]{2,1,0:T(8,128)(2,1)} %dbres_hbm.1, s32[4]{0:T(128)} %dblen_ref.1, s32[4]{0:T(128)} %seq_ref.1, ...), custom_call_target="tpu_custom_call" | custom-call | tf_op jit(solution)/shard_map/pallas_call | solution.py:239
  35.3 0.0 copy-start
  35.4 1.3 %slice_reduce_fusion = f32[16]{0:T(128)} fusion(f32[16,128]{1,0:T(8,128)} %get-tuple-element.4), kind=kLoop, calls=%fused_computation | loop fusion | bytes 128 | tf_op jit(solution)/shard_map/slice | solution.py:268
  36.7 0.0 copy-done
  36.7 0.6 %slice_reduce_fusion.1 = f32[4]{0:T(128)} fusion(f32[4,128]{1,0:T(4,128)S(1)} %copy-done), kind=kLoop, calls=%fused_computation.1 | loop fusion | bytes 32 | tf_op jit(solution)/shard_map/slice | solution.py:268
Async XLA Ops:
  35.3 1.3 %copy-start = (f32[4,128]{1,0:T(4,128)S(1)}, f32[4,128]{1,0:T(4,128)}, u32[]{:S(2)}) copy-start(f32[4,128]{1,0:T(4,128)} %get-tuple-element.5) | copy-start | bytes 6148

commit v3 on v2

--- a/solution.py
+++ b/solution.py
@@ -45,7 +45,7 @@
     coarse_ref, score_ref,
     qp_all, dbp, dbres, res_all, len_all, stat, stat_db, stat_node,
     local_sem, qp_send, qp_recv, len_send, len_recv, res_send, res_recv,
-    a_send, a_recv, b_send, b_recv,
+    a_send, a_recv, b_send, b_recv, share_send, share_recv,
 ):
     db, sub, rep = lax.axis_index("db"), lax.axis_index("sub"), lax.axis_index("rep")
     node = n_sub * n_rep
@@ -78,11 +78,25 @@
         len_all[db * held + q] = jnp.full(len_all.shape[1:], qlen_ref[q], jnp.int32)
     pl.semaphore_wait(barrier, n - 1 + node - 1)
 
+    half = width // n_rep
+
+    def columns(core):
+        return pl.ds(pl.multiple_of(core * half, LANES), half)
+
     def qp_copy(source, target, i):
-        return pltpu.make_async_remote_copy(
-            src_ref=qp_all.at[source], dst_ref=qp_all.at[source],
+        part = qp_all.at[source, :, columns(rep)]
+        return pltpu.make_async_remote_copy(
+            src_ref=part, dst_ref=part,
             send_sem=qp_send.at[i], recv_sem=qp_recv.at[source],
             device_id={"db": target}, device_id_type=MESH,
+        )
+
+    def share_copy(source, core, i):
+        part = qp_all.at[source, :, columns(core)]
+        return pltpu.make_async_remote_copy(
+            src_ref=part, dst_ref=part,
+            send_sem=share_send.at[i], recv_sem=share_recv.at[source],
+            device_id={"rep": 1 - rep}, device_id_type=MESH,
         )
 
     def len_copy(source, target, i):
@@ -131,6 +145,9 @@
     local[1].wait()
     for i in range(1, n):
         qp_copy(on_line(i), db, i).wait_recv()
+        share_copy(on_line(i), rep, i).start()
+    for i in range(1, n):
+        share_copy(on_line(i), 1 - rep, i).wait_recv()
     similar = lax.dot_general(
         qp_all[...].reshape(n * per_owner, width), dbp[...], (((1,), (1,)), ((), ())),
         preferred_element_type=jnp.float32,
@@ -202,6 +219,7 @@
 
     for i in range(1, n):
         qp_copy(db, on_line(i), i).wait_send()
+        share_copy(on_line(i), rep, i).wait_send()
         len_copy(db, on_line(i), i).wait_send()
         a_copy(db, on_line(i), i).wait_send()
     for i in range(1, node):
@@ -256,7 +274,7 @@
             dma((3,)),
             dma((n,)), dma((n,)), dma((n,)), dma((n,)),
             dma((2, n, held)), dma((n, held)),
-            dma((n,)), dma((n,)), dma((node,)), dma((node,)),
+            dma((n,)), dma((n,)), dma((node,)), dma((node,)), dma((n,)), dma((n,)),
         ],
         compiler_params=pltpu.CompilerParams(
             collective_id=0, has_side_effects=True, vmem_limit_bytes=60 * 2**20

time: 37.5 us -> 36.1 us (0.963)
  Pallas kernels: 34.7 us -> 33.3 us
    pallas_call x1, Pallas kernels: 34.7 us -> 33.3 us  [body(): pl.pallas_call(functools.partial(kernel, n, n_sub, n_rep), out_shape=(jax...]
where the time goes in v3:
time: 36.1 us; the launch traced here: 35.9 us
  Pallas kernels  33.3 us (92%)
  local copies, waits for them, and re-layouts  1.95 us (5%)
  between operations  0.65 us (2%)
    pallas_call x1, Pallas kernels, body(): pl.pallas_call(functools.partial(kernel, n, n_sub, n_rep), out_shape=(jax...  33.3 us
    slice x2, local copies, waits for them, and re-layouts, body(): return (coarse[:, 0], score[:, 0])  1.95 us

profile of v3, /device:TPU:0, one launch (start us, length us, event | category | flops | bytes accessed | tf_op | source)
XLA Modules:
  0.0 35.9 jit_solution(9248350565599728140)
XLA Ops:
  0.6 33.3 %shard_map.104 = (f32[16,128]{1,0:T(8,128)}, f32[4,128]{1,0:T(4,128)}) custom-call(bf16[16,1280]{1,0:T(8,128)(2,1)} %qp_ref.1, bf16[256,1280]{1,0:T(8,128)(2,1)} %dbp_hbm.1, bf16[2,64,1280]{2,1,0:T(8,128)(2,1)} %qres_hbm.1, s32[2]{0:T(128)} %qlen_ref.1, bf16[4,64,1280]{2,1,0:T(8,128)(2,1)} %dbres_hbm.1, s32[4]{0:T(128)} %dblen_ref.1, s32[4]{0:T(128)} %seq_ref.1, ...), custom_call_target="tpu_custom_call" | custom-call | tf_op jit(solution)/shard_map/pallas_call | solution.py:257
  33.9 0.0 copy-start
  33.9 1.3 %slice_reduce_fusion = f32[16]{0:T(128)} fusion(f32[16,128]{1,0:T(8,128)} %get-tuple-element.4), kind=kLoop, calls=%fused_computation | loop fusion | bytes 128 | tf_op jit(solution)/shard_map/slice | solution.py:286
  35.2 0.0 copy-done
  35.2 0.6 %slice_reduce_fusion.1 = f32[4]{0:T(128)} fusion(f32[4,128]{1,0:T(4,128)S(1)} %copy-done), kind=kLoop, calls=%fused_computation.1 | loop fusion | bytes 32 | tf_op jit(solution)/shard_map/slice | solution.py:286
Async XLA Ops:
  33.9 1.3 %copy-start = (f32[4,128]{1,0:T(4,128)S(1)}, f32[4,128]{1,0:T(4,128)}, u32[]{:S(2)}) copy-start(f32[4,128]{1,0:T(4,128)} %get-tuple-element.5) | copy-start | bytes 6148

commit v4 on v3

--- a/solution.py
+++ b/solution.py
@@ -190,12 +190,15 @@
         for i in range(1, node):
             b_copy(in_node(i)[0], in_node(i)[1], i).wait_recv()
         top, total = fold([(stat_node[k, 0], stat_node[k, 1]) for k in range(node)])
-        coarse_ref[...] = top + jnp.log(total)
+        value = top + jnp.log(total)
+        square = [lax.broadcasted_iota(jnp.int32, value.shape, d) for d in range(2)]
+        value = jnp.sum(jnp.where(square[0] == square[1], value, 0.0), axis=0, keepdims=True)
+        coarse_ref[...] = value[:, :per_owner]
 
     relay(1)
-    join_db()
     if n > 2:
         relay(2)
+    join_db()
     join_node()
     if n > 3:
         lax.fori_loop(3, n, lambda step, _: (relay(step), 0)[1], 0)
@@ -207,10 +210,12 @@
         chosen = dest_ref[c] * held + cq_ref[c]
         seq = seq_ref[c]
         value = align(res_all[chosen], dbres[seq], len_all[chosen][:1], dblen_ref[seq], factor)
-        score_ref[pl.ds(c, 1), :] = jnp.broadcast_to(value, (1, LANES))
+        lane = lax.broadcasted_iota(jnp.int32, score_ref.shape, 1)
+        score_ref[...] = jnp.where(lane == c, value, score_ref[...])
         return 0
 
-    count = score_ref.shape[0]
+    count = score_ref.shape[1]
+    score_ref[...] = jnp.zeros_like(score_ref)
     if count <= 8:
         for c in range(count):
             score(c, 0)
@@ -257,8 +262,8 @@
     coarse, score = pl.pallas_call(
         functools.partial(kernel, n, n_sub, n_rep),
         out_shape=(
-            jax.ShapeDtypeStruct((per_owner, LANES), jnp.float32),
-            jax.ShapeDtypeStruct((count, LANES), jnp.float32),
+            jax.ShapeDtypeStruct((1, per_owner), jnp.float32),
+            jax.ShapeDtypeStruct((1, count), jnp.float32),
         ),
         in_specs=[vmem, anywhere, anywhere, smem, anywhere, smem, smem, smem, smem],
         out_specs=(vmem, vmem),
@@ -283,7 +288,7 @@
         query_pooled, db_pooled, query_res, query_len, db_res, db_len,
         cand_seq, cand_dest[:, 0], cand_query,
     )
-    return coarse[:, 0], score[:, 0]
+    return coarse[0], score[0]
 
 
 def solution(mesh):

time: 36.1 us -> 35.9 us (level)
    slice x2 -> x0, local copies, waits for them, and re-layouts: 1.95 us -> none  [body(): return (coarse[:, 0], score[:, 0])]
    unnamed x2 -> x6, local copies, waits for them, and re-layouts: 0.01 us -> 1.8 us
where the time goes in v4:
time: 35.9 us; the launch traced here: 35.7 us
  Pallas kernels  33.2 us (92%)
  local copies, waits for them, and re-layouts  1.8 us (5%)
  between operations  0.65 us (2%)
    pallas_call x1, Pallas kernels, body(): pl.pallas_call(functools.partial(kernel, n, n_sub, n_rep), out_shape=(jax...  33.2 us
    unnamed x6, local copies, waits for them, and re-layouts  1.8 us

profile of v4, /device:TPU:0, one launch (start us, length us, event | category | flops | bytes accessed | tf_op | source)
XLA Modules:
  0.0 35.7 jit_solution(12480998864248676723)
XLA Ops:
  0.6 33.2 %shard_map.104 = (f32[1,16]{1,0:T(1,128)}, f32[1,4]{1,0:T(1,128)}) custom-call(bf16[16,1280]{1,0:T(8,128)(2,1)} %qp_ref.1, bf16[256,1280]{1,0:T(8,128)(2,1)} %dbp_hbm.1, bf16[2,64,1280]{2,1,0:T(8,128)(2,1)} %qres_hbm.1, s32[2]{0:T(128)} %qlen_ref.1, bf16[4,64,1280]{2,1,0:T(8,128)(2,1)} %dbres_hbm.1, s32[4]{0:T(128)} %dblen_ref.1, s32[4]{0:T(128)} %seq_ref.1, ...), custom_call_target="tpu_custom_call" | custom-call | tf_op jit(solution)/shard_map/pallas_call | solution.py:262
  33.9 0.0 copy-start.1
  33.9 0.7 %copy-done.1 = f32[1,16]{1,0:T(1,128)S(1)} copy-done((f32[1,16]{1,0:T(1,128)S(1)}, f32[1,16]{1,0:T(1,128)}, u32[]{:S(2)}) %copy-start.1) | copy-done | bytes 88
  34.5 0.0 copy-start
  34.5 0.5 %copy.13 = f32[16]{0:T(128)} copy(f32[16]{0:T(128)S(1)} %bitcast.5) | data formatting | bytes 128
  35.1 0.1 copy-done
  35.2 0.5 %copy.14 = f32[4]{0:T(128)} copy(f32[4]{0:T(128)S(1)} %bitcast.4) | data formatting | bytes 32
Async XLA Ops:
  33.9 0.7 %copy-start.1 = (f32[1,16]{1,0:T(1,128)S(1)}, f32[1,16]{1,0:T(1,128)}, u32[]{:S(2)}) copy-start(f32[1,16]{1,0:T(1,128)} %get-tuple-element.4) | copy-start | bytes 196
  34.5 0.6 %copy-start = (f32[1,4]{1,0:T(1,128)S(1)}, f32[1,4]{1,0:T(1,128)}, u32[]{:S(2)}) copy-start(f32[1,4]{1,0:T(1,128)} %get-tuple-element.5) | copy-start | bytes 52
